TPU v7x, 128 devices: a whole 4x4x4 slice. The times are simulated.
128 devices in a mesh: frame: 64 (over x, z, y), head: 2 (over core).
Axes of the slice: x: 4, y: 4, z: 4, core: 2. Of those that a mesh axis runs over, the one named last changes fastest.
Arguments:
- queries: bfloat16 [32768, 3072], P('frame', 'head'), may hold values from -8 to 8
- key_rows: bfloat16 [32768, 3072], P('frame', 'head'), may hold values from -8 to 8
- value_rows: bfloat16 [32768, 3072], P('frame', 'head'), may hold values from -6 to 6
- block_mask: int32 [512, 32], P('frame'), may hold values from -1 to 511, as said below
- out_weight: bfloat16 [3072, 3072], P('head'), may hold values from -0.109375 to 0.109375
Outputs:
- attended: bfloat16 [32768, 3072], P(('frame', 'head'))
Inputs may be any that keep to these rules, and one draw needn't show every extreme that they name: `block_mask`: row f * 8 + b belongs to block b of frame f. Its first 8 entries are the blocks of frame f in order. Entry 8 + 4 k + 2 s + r, for k below 6 and r of 0 and 1, names a block of frame f - 2^k (s = 0) or f + 2^k (s = 1), or is -1 exactly when that frame lies outside the clip; its two entries r differ. Over the 8 rows of one frame, the entries of one k and s name exactly max(2, 8 // 2^k) different blocks.
All inputs are finite; a program needn't handle non-finite values.
Results may differ from a plain program's by a relative error of at most 0.0058.
Values may be sent and summed in bfloat16 or wider, within the bound.
No kernel may reach another device: no remote copies, remote signals or barrier semaphores. Data moves between devices by JAX's collectives and lax.ppermute only.
A program may use at most 192 MiB of HBM per device.

v0:
```python
import math

import jax
import jax.numpy as jnp
from jax import lax
from jax.sharding import PartitionSpec as P

HD = 128
BLK = 64


def shifted(value, axis, steps):
    count = lax.axis_size(axis)
    leading, last = (max(0, -steps), min(count, count - steps))
    return lax.ppermute(value, axis, [(source, source + steps) for source in range(leading, last)])


def on_device(queries, key_rows, value_rows, block_mask, out_weight):
    frames = lax.axis_size("frame")
    position = lax.axis_index("frame")
    tok_rows, features = queries.shape
    per_block = BLK
    blocks = tok_rows // per_block
    local_heads = features // HD
    slot_count = block_mask.shape[1]
    levels = frames.bit_length() - 1
    paired = jnp.concatenate([key_rows, value_rows], axis=1).reshape(
        blocks, per_block, 2 * features
    )
    slots_all = jnp.arange(blocks, dtype=jnp.int32)
    pieces = [paired]
    columns = [jnp.broadcast_to(slots_all[None, :], (blocks, blocks))]
    filled = blocks
    for octave in range(levels):
        distance = 2**octave
        for direction in range(2):
            offset = (2 * direction - 1) * distance
            leading = blocks + 4 * octave + 2 * direction
            named_blocks = block_mask[:, leading : leading + 2]
            usable = named_blocks >= 0
            local_index = jnp.where(usable, named_blocks - (position + offset) * blocks, 0)
            received = shifted(paired, "frame", -offset)
            pieces.append(received)
            columns.append(jnp.where(usable, filled + local_index, 0))
            filled += blocks
    slot_index = jnp.concatenate(columns, axis=1)
    candidate = jnp.concatenate(pieces, axis=0)
    slot_valid = block_mask >= 0
    inv_root = 1.0 / math.sqrt(HD)

    def attend_block(operands):
        qblock, slot_row, slot_ok = operands
        gathered = candidate[slot_row]
        key_part = gathered[:, :, :features].reshape(slot_count, per_block, local_heads, HD)
        value_part = gathered[:, :, features:].reshape(slot_count, per_block, local_heads, HD)
        scores = (
            jnp.einsum("qhd,sbhd->hqsb", qblock, key_part, preferred_element_type=jnp.float32)
            * inv_root
        )
        scores = jnp.where(slot_ok[None, None, :, None], scores, -jnp.inf)
        peak = jnp.max(scores, axis=(2, 3), keepdims=True)
        raised = jnp.exp(scores - peak)
        total = jnp.sum(raised, axis=(2, 3), keepdims=True)
        weights = (raised / total).astype(jnp.bfloat16)
        mixed = jnp.einsum(
            "hqsb,sbhd->qhd", weights, value_part, preferred_element_type=jnp.float32
        )
        return mixed.astype(jnp.bfloat16).reshape(per_block, features)

    query_blocks = queries.reshape(blocks, per_block, local_heads, HD)
    heads_out = lax.map(attend_block, (query_blocks, slot_index, slot_valid)).reshape(
        tok_rows, features
    )
    summed = lax.psum_scatter(
        jnp.dot(heads_out, out_weight, preferred_element_type=jnp.float32),
        "head",
        scatter_dimension=0,
        tiled=True,
    )
    return summed.astype(jnp.bfloat16)


def solution(mesh):
    in_specs = (
        P("frame", "head"),
        P("frame", "head"),
        P("frame", "head"),
        P("frame", None),
        P("head", None),
    )
    out_specs = P(("frame", "head"), None)
    return jax.shard_map(
        on_device, mesh=mesh, in_specs=in_specs, out_specs=out_specs, check_vma=False
    )
```

profile of v0, /device:TPU:1, one launch (start us, length us, event | category | flops | bytes accessed | tf_op | source)
XLA Modules:
  0.0 996.9 jit_solution(6879907835129321304)
XLA Ops:
  29.9 49.7 %collective-permute-done = bf16[8,64,3072]{2,1,0:T(8,128)(2,1)S(1)} collective-permute-done((bf16[8,64,3072]{2,1,0:T(8,128)(2,1)S(1)}, bf16[8,64,3072]{2,1,0:T(8,128)(2,1)S(1)}, u32[]{:S(2)}, u32[]{:S(2)}) %collective-permute-start) | collective-permute-done | bytes 3145760 | tf_op jit(solution)/shard_map/ppermute | solution.py:15
  80.8 70.1 %collective-permute-done.1 = bf16[8,64,3072]{2,1,0:T(8,128)(2,1)S(1)} collective-permute-done((bf16[8,64,3072]{2,1,0:T(8,128)(2,1)S(1)}, bf16[8,64,3072]{2,1,0:T(8,128)(2,1)S(1)}, u32[]{:S(2)}, u32[]{:S(2)}) %collective-permute-start.1) | collective-permute-done | bytes 3145760 | tf_op jit(solution)/shard_map/ppermute | solution.py:15
  167.4 50.5 %collective-permute-done.3 = bf16[8,64,3072]{2,1,0:T(8,128)(2,1)} collective-permute-done((bf16[8,64,3072]{2,1,0:T(8,128)(2,1)S(1)}, bf16[8,64,3072]{2,1,0:T(8,128)(2,1)}, u32[]{:S(2)}, u32[]{:S(2)}) %collective-permute-start.3) | collective-permute-done | bytes 3145760 | tf_op jit(solution)/shard_map/ppermute | solution.py:15
  217.9 52.2 %collective-permute-start.8 = (bf16[8,64,3072]{2,1,0:T(8,128)(2,1)S(1)}, bf16[8,64,3072]{2,1,0:T(8,128)(2,1)S(1)}, u32[]{:S(2)}, u32[]{:S(2)}) collective-permute-start(bf16[8,64,3072]{2,1,0:T(8,128)(2,1)S(1)} %bitcast.100), channel_id=1, source_target_pairs={{0,32},{2,34},{4,36},{6,38},{8,40},{10,42},{12,44},{14,46},{16,48}... | collective-permute-start | bytes 9437192 | tf_op jit(solution)/shard_map/ppermute | solution.py:15
  279.0 124.0 %collective-permute-start.10 = (bf16[8,64,3072]{2,1,0:T(8,128)(2,1)S(1)}, bf16[8,64,3072]{2,1,0:T(8,128)(2,1)S(1)}, u32[]{:S(2)}, u32[]{:S(2)}) collective-permute-start(bf16[8,64,3072]{2,1,0:T(8,128)(2,1)S(1)} %bitcast.102), channel_id=1, source_target_pairs={{0,64},{2,66},{4,68},{6,70},{8,72},{10,74},{12,76},{14,78},{16,80}... | collective-permute-start | bytes 9437192 | tf_op jit(solution)/shard_map/ppermute | solution.py:15
  428.8 97.7 %collective-permute-done.9 = bf16[8,64,3072]{2,1,0:T(8,128)(2,1)S(1)} collective-permute-done((bf16[8,64,3072]{2,1,0:T(8,128)(2,1)S(1)}, bf16[8,64,3072]{2,1,0:T(8,128)(2,1)S(1)}, u32[]{:S(2)}, u32[]{:S(2)}) %collective-permute-start.9) | collective-permute-done | bytes 3145760 | tf_op jit(solution)/shard_map/ppermute | solution.py:15
  532.1 338.3 %while.10 = (s32[]{:T(128)}, bf16[8,64,1536]{2,1,0:T(8,128)(2,1)}, s32[8,32]{1,0:T(8,128)S(1)}, bf16[104,64,3072]{2,1,0:T(8,128)(2,1)}, pred[8,32]{1,0:T(8,128)(...) while((s32[]{:T(128)}, bf16[8,64,1536]{2,1,0:T(8,128)(2,1)}, s32[8,32]{1,0:T(8,128)S(1)}, ...), condition=%wide.region_3.4_spmd, body=%wide.region_0.3_spmd.sunk | while | flops 824278656 | bytes 127428360 | solution.py:71
  532.1 9.6 gather_fusion
  541.6 9.6 slice_bitcast_fusion.3
  563.4 9.8 fusion.38
  574.3 9.7 gather_fusion
  584.0 9.6 slice_bitcast_fusion.3
  605.8 9.8 fusion.38
  616.6 9.7 gather_fusion
  626.3 9.6 slice_bitcast_fusion.3
  648.1 9.8 fusion.38
  658.9 9.7 gather_fusion
  668.6 9.6 slice_bitcast_fusion.3
  690.4 9.8 fusion.38
  710.8 9.6 slice_bitcast_fusion.3
  732.6 9.8 fusion.38
  743.4 9.7 gather_fusion
  753.1 9.6 slice_bitcast_fusion.3
  774.9 9.8 fusion.38
  785.8 9.7 gather_fusion
  795.4 9.6 slice_bitcast_fusion.3
  817.2 9.8 fusion.38
  828.0 9.7 gather_fusion
  837.7 9.6 slice_bitcast_fusion.3
  859.5 9.8 fusion.38
  870.3 9.8 fusion.23
  880.2 106.6 %reduce-scatter.2.cloned.1.call-done = f32[256,3072]{1,0:T(8,128)} async-done(((f32[512,3072]{1,0:T(8,128)}), f32[256,3072]{1,0:T(8,128)}) %reduce-scatter.2.cloned.1.call-update) | async-done | bytes 3145744 | tf_op jit(solution)/shard_map/reduce_scatter | solution.py:74
  (138 shorter events, 199.4 us)
Async XLA Ops:
  6.5 153.5 %copy-start.3 = (s32[8,32]{1,0:T(8,128)S(1)}, s32[8,32]{1,0:T(8,128)}, u32[]{:S(2)}) copy-start(s32[8,32]{1,0:T(8,128)} %param.10) | copy-start | bytes 3076
  6.5 980.3 %reduce-scatter.2.cloned.1.call-start = ((), (), s32[]{:S(2)}) async-start(), calls=%async_computation.1 | async-start | bytes 9437184 | tf_op jit(solution)/shard_map/reduce_scatter | solution.py:74
  8.8 70.8 %collective-permute-start = (bf16[8,64,3072]{2,1,0:T(8,128)(2,1)S(1)}, bf16[8,64,3072]{2,1,0:T(8,128)(2,1)S(1)}, u32[]{:S(2)}, u32[]{:S(2)}) collective-permute-start(bf16[8,64,3072]{2,1,0:T(8,128)(2,1)S(1)} %bitcast.91), channel_id=1, source_target_pairs={{0,2},{2,4},{4,6},{6,8},{8,10},{10,12},{12,14},{14,16},{16,18},{18... | collective-permute-start | bytes 9437192 | tf_op jit(solution)/shard_map/ppermute | solution.py:15
  13.0 138.0 %collective-permute-start.1 = (bf16[8,64,3072]{2,1,0:T(8,128)(2,1)S(1)}, bf16[8,64,3072]{2,1,0:T(8,128)(2,1)S(1)}, u32[]{:S(2)}, u32[]{:S(2)}) collective-permute-start(bf16[8,64,3072]{2,1,0:T(8,128)(2,1)S(1)} %bitcast.92), channel_id=1, source_target_pairs={{2,0},{4,2},{6,4},{8,6},{10,8},{12,10},{14,12},{16,14},{18,16},{20... | collective-permute-start | bytes 9437192 | tf_op jit(solution)/shard_map/ppermute | solution.py:15
  14.3 144.4 %collective-permute-start.2 = (bf16[8,64,3072]{2,1,0:T(8,128)(2,1)S(1)}, bf16[8,64,3072]{2,1,0:T(8,128)(2,1)}, u32[]{:S(2)}, u32[]{:S(2)}) collective-permute-start(bf16[8,64,3072]{2,1,0:T(8,128)(2,1)S(1)} %bitcast.93), channel_id=1, source_target_pairs={{0,4},{2,6},{4,8},{6,10},{8,12},{10,14},{12,16},{14,18},{16,20},{1... | collective-permute-start | bytes 9437192 | tf_op jit(solution)/shard_map/ppermute | solution.py:15
  21.4 196.5 %collective-permute-start.3 = (bf16[8,64,3072]{2,1,0:T(8,128)(2,1)S(1)}, bf16[8,64,3072]{2,1,0:T(8,128)(2,1)}, u32[]{:S(2)}, u32[]{:S(2)}) collective-permute-start(bf16[8,64,3072]{2,1,0:T(8,128)(2,1)S(1)} %bitcast.94), channel_id=1, source_target_pairs={{4,0},{6,2},{8,4},{10,6},{12,8},{14,10},{16,12},{18,14},{20,16},{2... | collective-permute-start | bytes 9437192 | tf_op jit(solution)/shard_map/ppermute | solution.py:15
  22.7 251.2 %collective-permute-start.4 = (bf16[8,64,3072]{2,1,0:T(8,128)(2,1)S(1)}, bf16[8,64,3072]{2,1,0:T(8,128)(2,1)}, u32[]{:S(2)}, u32[]{:S(2)}) collective-permute-start(bf16[8,64,3072]{2,1,0:T(8,128)(2,1)S(1)} %bitcast.95), channel_id=1, source_target_pairs={{0,8},{2,10},{4,12},{6,14},{8,16},{10,18},{12,20},{14,22},{16,24},... | collective-permute-start | bytes 9437192 | tf_op jit(solution)/shard_map/ppermute | solution.py:15
  79.6 76.1 %copy-start.2 = (bf16[8,64,3072]{2,1,0:T(8,128)(2,1)}, bf16[8,64,3072]{2,1,0:T(8,128)(2,1)S(1)}, u32[]{:S(2)}) copy-start(bf16[8,64,3072]{2,1,0:T(8,128)(2,1)S(1)} %collective-permute-done) | copy-start | bytes 9437188
  79.6 199.5 %collective-permute-start.5 = (bf16[8,64,3072]{2,1,0:T(8,128)(2,1)S(1)}, bf16[8,64,3072]{2,1,0:T(8,128)(2,1)}, u32[]{:S(2)}, u32[]{:S(2)}) collective-permute-start(bf16[8,64,3072]{2,1,0:T(8,128)(2,1)S(1)} %bitcast.96), channel_id=1, source_target_pairs={{8,0},{10,2},{12,4},{14,6},{16,8},{18,10},{20,12},{22,14},{24,16},... | collective-permute-start | bytes 9437192 | tf_op jit(solution)/shard_map/ppermute | solution.py:15
  151.0 1.6 copy-start.1
  152.6 254.2 %collective-permute-start.6 = (bf16[8,64,3072]{2,1,0:T(8,128)(2,1)S(1)}, bf16[8,64,3072]{2,1,0:T(8,128)(2,1)}, u32[]{:S(2)}, u32[]{:S(2)}) collective-permute-start(bf16[8,64,3072]{2,1,0:T(8,128)(2,1)S(1)} %bitcast.97), channel_id=1, source_target_pairs={{0,16},{2,18},{4,20},{6,22},{8,24},{10,26},{12,28},{14,30},{16,32}... | collective-permute-start | bytes 9437192 | tf_op jit(solution)/shard_map/ppermute | solution.py:15
  158.7 264.3 %collective-permute-start.7 = (bf16[8,64,3072]{2,1,0:T(8,128)(2,1)S(1)}, bf16[8,64,3072]{2,1,0:T(8,128)(2,1)}, u32[]{:S(2)}, u32[]{:S(2)}) collective-permute-start(bf16[8,64,3072]{2,1,0:T(8,128)(2,1)S(1)} %bitcast.99), channel_id=1, source_target_pairs={{16,0},{18,2},{20,4},{22,6},{24,8},{26,10},{28,12},{30,14},{32,16}... | collective-permute-start | bytes 9437192 | tf_op jit(solution)/shard_map/ppermute | solution.py:15
  217.9 209.0 %collective-permute-start.8 = (bf16[8,64,3072]{2,1,0:T(8,128)(2,1)S(1)}, bf16[8,64,3072]{2,1,0:T(8,128)(2,1)S(1)}, u32[]{:S(2)}, u32[]{:S(2)}) collective-permute-start(bf16[8,64,3072]{2,1,0:T(8,128)(2,1)S(1)} %bitcast.100), channel_id=1, source_target_pairs={{0,32},{2,34},{4,36},{6,38},{8,40},{10,42},{12,44},{14,46},{16,48}... | collective-permute-start | bytes 9437192 | tf_op jit(solution)/shard_map/ppermute | solution.py:15
  273.9 252.6 %collective-permute-start.9 = (bf16[8,64,3072]{2,1,0:T(8,128)(2,1)S(1)}, bf16[8,64,3072]{2,1,0:T(8,128)(2,1)S(1)}, u32[]{:S(2)}, u32[]{:S(2)}) collective-permute-start(bf16[8,64,3072]{2,1,0:T(8,128)(2,1)S(1)} %bitcast.101), channel_id=1, source_target_pairs={{32,0},{34,2},{36,4},{38,6},{40,8},{42,10},{44,12},{46,14},{48,16}... | collective-permute-start | bytes 9437192 | tf_op jit(solution)/shard_map/ppermute | solution.py:15
  279.0 249.3 %collective-permute-start.10 = (bf16[8,64,3072]{2,1,0:T(8,128)(2,1)S(1)}, bf16[8,64,3072]{2,1,0:T(8,128)(2,1)S(1)}, u32[]{:S(2)}, u32[]{:S(2)}) collective-permute-start(bf16[8,64,3072]{2,1,0:T(8,128)(2,1)S(1)} %bitcast.102), channel_id=1, source_target_pairs={{0,64},{2,66},{4,68},{6,70},{8,72},{10,74},{12,76},{14,78},{16,80}... | collective-permute-start | bytes 9437192 | tf_op jit(solution)/shard_map/ppermute | solution.py:15
  406.8 123.5 %collective-permute-start.11 = (bf16[8,64,3072]{2,1,0:T(8,128)(2,1)S(1)}, bf16[8,64,3072]{2,1,0:T(8,128)(2,1)S(1)}, u32[]{:S(2)}, u32[]{:S(2)}) collective-permute-start(bf16[8,64,3072]{2,1,0:T(8,128)(2,1)S(1)} %bitcast.103), channel_id=1, source_target_pairs={{64,0},{66,2},{68,4},{70,6},{72,8},{74,10},{76,12},{78,14},{80,16}... | collective-permute-start | bytes 9437192 | tf_op jit(solution)/shard_map/ppermute | solution.py:15
  555.9 4.6 copy-start
  598.3 4.6 copy-start
  640.5 4.6 copy-start
  682.8 4.6 copy-start
  725.0 4.6 copy-start
  767.4 4.6 copy-start
  809.7 4.6 copy-start
  852.0 4.6 copy-start
Sparse Core Ops, SparseCore 0:
  880.3 106.4 reduce-scatter.1
where the time goes:
time: 998 us; the launch traced here: 997 us
  waiting for transfers between devices  375 us (38%)
  local copies, waits for them, and re-layouts  262 us (26%)
  starting transfers between devices  205 us (21%)
  matrix products  111 us (11%)
  other arithmetic  30.4 us (3%)
  between operations  13.5 us (1%)
    ppermute x12, waiting for transfers between devices, shifted(): lax.ppermute(value, axis, [(source, source + steps) for source in range(l...  268 us
    ppermute x12, starting transfers between devices, shifted(): lax.ppermute(value, axis, [(source, source + steps) for source in range(l...  205 us
    while x24, local copies, waits for them, and re-layouts  113 us
    reduce_scatter x1, waiting for transfers between devices, on_device(): lax.psum_scatter(jnp.dot(heads_out, out_weight, preferred_element_type=jn...  107 us
    dot_general x8, matrix products, attend_block(): jnp.einsum('hqsb,sbhd->qhd', weights, value_part, preferred_element_type=...  78.4 us
    gather x8, local copies, waits for them, and re-layouts, attend_block(): gathered = candidate[slot_row]  77.3 us
    unnamed x18, local copies, waits for them, and re-layouts  39.4 us
    reduce_sum x8, other arithmetic, attend_block(): total = jnp.sum(raised, axis=(2, 3), keepdims=True)  23.6 us
  transfers between devices with their start and end apart: 13, of which 5 were waited for; matrix products, arithmetic and copies ran while one was open for 5% of the time, Pallas kernels for 0%

commit v1 on v0

v1 whole, which is shorter than its diff:
```python
import functools
import math

import jax
import jax.numpy as jnp
from jax import lax
from jax.experimental import pallas as pl
from jax.experimental.pallas import tpu as pltpu
from jax.sharding import PartitionSpec as P

HD = 128
BLK = 64
BF = 8
G = 4
SLOTS = 32
GB = G * BF
LOW = -1e30
C = math.log2(math.e) / math.sqrt(HD)
VMEM = 56 * 1024 * 1024
EXT = 26


def line_pairs(frames, shift):
    return [(f, f // G * G + (f + shift) % G) for f in range(frames)]


def group_pairs(frames, distance):
    return [(f, f + G * distance) for f in range(frames) if 0 <= f + G * distance < frames]


def swap_pairs(frames):
    return [(f, f ^ (frames // 2)) for f in range(frames)]


def softmax_part(q, k_ref, v_ref, bias_ref, first_block, blocks, start):
    keys = k_ref.shape[0]
    s = lax.dot_general(q, k_ref[...], (((1,), (1,)), ((), ())), preferred_element_type=jnp.float32)
    s = s.reshape(blocks, BLK, keys) * C
    s = s + bias_ref[pl.ds(first_block, blocks)]
    s = s.reshape(blocks * BLK, keys)
    peak = jnp.max(s, axis=1, keepdims=True)
    if start is not None:
        peak = jnp.maximum(peak, start)
    raised = jnp.exp2(s - peak)
    total = jnp.sum(raised, axis=1, keepdims=True)
    mixed = jnp.dot(raised.astype(jnp.bfloat16), v_ref[...], preferred_element_type=jnp.float32)
    return peak, total, mixed


QT = 4


def inner_kernel(q_ref, k_ref, v_ref, bias_ref, acc_ref, peak_ref, total_ref):
    rows = QT * BLK

    def step(t, _):
        at = pl.ds(pl.multiple_of(t * rows, rows), rows)
        peak, total, mixed = softmax_part(q_ref[at, :], k_ref, v_ref, bias_ref, t * QT, QT, None)
        acc_ref[at, :] = mixed
        peak_ref[at, :] = jnp.broadcast_to(peak, (rows, HD))
        total_ref[at, :] = jnp.broadcast_to(total, (rows, HD))
        return 0

    lax.fori_loop(0, q_ref.shape[0] // rows, step, 0)


def inner(q, kv, bias):
    tokens, features = q.shape
    heads = features // HD
    column = pl.BlockSpec((tokens, HD), lambda h: (0, h))
    shape = jax.ShapeDtypeStruct((tokens, features), jnp.float32)
    return pl.pallas_call(
        inner_kernel,
        grid=(heads,),
        in_specs=[
            column,
            column,
            pl.BlockSpec((tokens, HD), lambda h: (0, heads + h)),
            pl.BlockSpec(bias.shape, lambda h: (0, 0, 0)),
        ],
        out_specs=[column, column, column],
        out_shape=[shape, shape, shape],
        compiler_params=pltpu.CompilerParams(vmem_limit_bytes=VMEM),
        cost_estimate=pl.CostEstimate(
            flops=4 * tokens * tokens * features, bytes_accessed=16 * tokens * features, transcendentals=tokens * tokens * heads
        ),
    )(q, kv, kv, bias)


def outer_kernel(counts, table, q_ref, bias_ref, acc_ref, peak_ref, total_ref, *rest):
    pieces = rest[: len(counts)]
    out_ref, held, k_all, v_all, sems = rest[len(counts) :]
    heads = held.shape[2] // HD // 2
    head, slot = pl.program_id(0), pl.program_id(1)
    rows = QT * BLK

    @pl.when((head == 0) & (slot == 0))
    def _():
        copies = []
        begin = 0
        for i, (count, piece) in enumerate(zip(counts, pieces)):
            copies.append(pltpu.make_async_copy(piece, held.at[pl.ds(begin, count)], sems.at[i]))
            begin += count
        for copy in copies:
            copy.start()
        for copy in copies:
            copy.wait()

    for h in range(heads):

        @pl.when(head == h)
        def _():
            for e in range(EXT):
                block = table[slot * EXT + e]
                k_all[e * BLK : (e + 1) * BLK, :] = held[block, :, h * HD : (h + 1) * HD]
                v_all[e * BLK : (e + 1) * BLK, :] = held[block, :, (heads + h) * HD : (heads + h + 1) * HD]

    def step(t, _):
        at = pl.ds(pl.multiple_of(t * rows, rows), rows)
        before = peak_ref[at, :1]
        peak, total, mixed = softmax_part(q_ref[at, :], k_all, v_all, bias_ref, t * QT, QT, before)
        keep = jnp.exp2(before - peak)
        total = total + total_ref[at, :1] * keep
        out_ref[at, :] = ((mixed + acc_ref[at, :] * keep) / total).astype(out_ref.dtype)
        return 0

    lax.fori_loop(0, q_ref.shape[0] // rows, step, 0)


def outer(table, q, bias, partial, pieces):
    tokens, features = q.shape
    heads = features // HD
    rows = tokens // G
    counts = tuple(piece.shape[0] for piece in pieces)
    spec = pl.BlockSpec((rows, HD), lambda h, s, *_: (s, h))
    return pl.pallas_call(
        functools.partial(outer_kernel, counts),
        grid_spec=pltpu.PrefetchScalarGridSpec(
            num_scalar_prefetch=1,
            grid=(heads, G),
            in_specs=[
                spec,
                pl.BlockSpec((BF, 1, EXT * BLK), lambda h, s, *_: (s, 0, 0)),
                spec,
                spec,
                spec,
            ]
            + [pl.BlockSpec(memory_space=pl.ANY)] * len(pieces),
            out_specs=spec,
            scratch_shapes=[
                pltpu.VMEM((sum(counts), BLK, 2 * features), jnp.bfloat16),
                pltpu.VMEM((EXT * BLK, HD), jnp.bfloat16),
                pltpu.VMEM((EXT * BLK, HD), jnp.bfloat16),
                pltpu.SemaphoreType.DMA((len(counts),)),
            ],
        ),
        out_shape=jax.ShapeDtypeStruct((tokens, features), jnp.bfloat16),
        compiler_params=pltpu.CompilerParams(vmem_limit_bytes=VMEM),
        cost_estimate=pl.CostEstimate(
            flops=4 * tokens * EXT * BLK * features, bytes_accessed=16 * tokens * features, transcendentals=tokens * EXT * BLK * heads
        ),
    )(table.reshape(-1), q, bias, *partial, *pieces)


def named(mask, frame, y):
    return lax.dynamic_index_in_dim(mask, (y - frame) % G, 0, keepdims=False)


def distinct(entries, first, count):
    within = jnp.arange(BF, dtype=jnp.int32)
    present = jnp.any(entries.reshape(-1)[:, None] == (first + within)[None, :], axis=0)
    rank = jnp.cumsum(present.astype(jnp.int32))
    hit = present[None, :] & (rank[None, :] == 1 + jnp.arange(count, dtype=jnp.int32)[:, None])
    return first + jnp.sum(jnp.where(hit, within[None, :], 0), axis=1)


def requests(mask, a, y):
    within = jnp.arange(BF, dtype=jnp.int32)
    frames = [named(mask, i, y) for i in range(G)]
    below, above = (a - 1) * GB, (a + 1) * GB
    m1 = jnp.concatenate(
        [
            below + 3 * BF + within,
            distinct(frames[0][:, 12:14], below + 2 * BF, 4),
            frames[2][0, 16:18],
            frames[1][0, 16:18],
            frames[0][0, 16:18],
        ]
    )
    p1 = jnp.concatenate(
        [
            above + within,
            distinct(frames[3][:, 14:16], above + BF, 4),
            frames[1][0, 18:20],
            frames[2][0, 18:20],
            frames[3][0, 18:20],
        ]
    )
    far = [mask[:, 0, c : c + 2].reshape(-1) for c in (20, 22, 24, 26)]
    swap = jnp.maximum(mask[:, 0, 28:30], mask[:, 0, 30:32]).reshape(-1)
    return [m1, p1, *far, swap]


def on_device(queries, key_rows, value_rows, block_mask, out_weight):
    n = lax.axis_size("frame")
    position = lax.axis_index("frame")
    y, a = position % G, position // G
    tokens, features = queries.shape
    share = features // G

    def line(value, shift):
        return lax.ppermute(value, "frame", line_pairs(n, shift))

    def reach(distance):
        return swap_pairs(n) if distance == 8 else group_pairs(n, distance)

    def chunk(x, shift):
        return lax.dynamic_slice_in_dim(x, (y + shift) % G * share, share, 1)

    kv = [jnp.concatenate([chunk(key_rows, s), chunk(value_rows, s)], axis=1) for s in range(G)]
    kv = jnp.stack([kv[0]] + [line(kv[s], s) for s in (1, 2, 3)])
    q = jnp.concatenate([chunk(queries, 0)] + [line(chunk(queries, s), s) for s in (1, 2, 3)], axis=0)
    blocks = kv.reshape(GB, BLK, 2 * share)

    mask = jnp.stack([block_mask] + [line(block_mask, s) for s in (1, 2, 3)])
    wanted = requests(mask, a, y)
    sizes = [w.shape[0] for w in wanted]
    distances = (-1, 1, -2, 2, -4, 4, 8)
    pieces = []
    for w, d in zip(wanted, distances):
        asked = lax.ppermute(w, "frame", reach(d))
        local = jnp.clip(asked - a * GB, 0, GB - 1)
        index = (y - local // BF) % G * BF + local % BF
        back = 8 if d == 8 else -d
        pieces.append(lax.ppermute(blocks[index], "frame", reach(back)))

    rows = mask.reshape(GB, SLOTS)
    slots = jnp.arange(G, dtype=jnp.int32)
    frame_of = (y - slots) % G
    ids = (a * GB + frame_of[:, None] * BF + jnp.arange(BF, dtype=jnp.int32)[None, :]).reshape(-1)
    hit = jnp.any(rows[:, :, None] == ids[None, None, :], axis=1)
    bias_in = jnp.repeat(jnp.where(hit, 0.0, LOW), BLK, axis=1)[:, None, :]

    starts = [sum(sizes[:i]) for i in range(len(sizes))]
    m1, p1 = starts[0], starts[1]
    flat = jnp.concatenate(wanted)
    three = mask[(y - 3) % G, 0, 16:18] - ((a - 1) * GB + 3 * BF)
    zero = mask[y % G, 0, 18:20] - (a + 1) * GB
    within = jnp.arange(BF, dtype=jnp.int32)
    none = jnp.full((4,), -1, jnp.int32)
    four = jnp.arange(4, dtype=jnp.int32)
    two = jnp.arange(2, dtype=jnp.int32)
    tables = jnp.stack(
        [
            jnp.concatenate([m1 + within, m1 + 8 + four, m1 + 16 + two, p1 + jnp.clip(zero, 0, BF - 1)]),
            jnp.concatenate([m1 + within, none, m1 + 14 + two, p1 + 12 + two]),
            jnp.concatenate([p1 + within, none, m1 + 12 + two, p1 + 14 + two]),
            jnp.concatenate([p1 + within, p1 + 8 + four, m1 + jnp.clip(three, 0, BF - 1), p1 + 16 + two]),
        ]
    )[frame_of]
    far = jnp.concatenate(
        [start + 2 * slots[:, None] + two[None, :] for start in starts[2:]], axis=1
    )
    table = jnp.concatenate([tables, far], axis=1)
    held = jnp.where(table >= 0, flat[jnp.maximum(table, 0)], -1)
    hit = (rows.reshape(G, BF, SLOTS, 1) == held[:, None, None, :]) & (held >= 0)[:, None, None, :]
    hit = jnp.any(hit, axis=2).reshape(GB, EXT)
    bias_out = jnp.repeat(jnp.where(hit, 0.0, LOW), BLK, axis=1)[:, None, :]

    partial = inner(q, kv.reshape(G * tokens, 2 * share), bias_in)
    heads_out = outer(jnp.maximum(table, 0), q, bias_out, partial, pieces).reshape(G, tokens, share)

    mixed = jnp.concatenate([heads_out[0]] + [line(heads_out[G - s], s) for s in (1, 2, 3)], axis=1)
    weight = jnp.concatenate(
        [lax.dynamic_slice_in_dim(out_weight, (y - s) % G * share, share, 0) for s in range(G)], axis=0
    )
    half = tokens // 2
    core = lax.axis_index("head")
    theirs = lax.dynamic_slice_in_dim(mixed, (1 - core) * half, half, 0)
    ours = lax.dynamic_slice_in_dim(mixed, core * half, half, 0)
    sent = jnp.dot(theirs, weight, preferred_element_type=jnp.float32).astype(jnp.bfloat16)
    other = lax.ppermute(sent, "head", [(0, 1), (1, 0)])
    kept = jnp.dot(ours, weight, preferred_element_type=jnp.float32)
    return (kept + other.astype(jnp.float32)).astype(jnp.bfloat16)


def solution(mesh):
    in_specs = (
        P("frame", "head"),
        P("frame", "head"),
        P("frame", "head"),
        P("frame", None),
        P("head", None),
    )
    out_specs = P(("frame", "head"), None)
    return jax.shard_map(
        on_device, mesh=mesh, in_specs=in_specs, out_specs=out_specs, check_vma=False
    )
```

time: 998 us -> 266 us (0.27)
  waiting for transfers between devices: 375 us -> 32.4 us
  local copies, waits for them, and re-layouts: 262 us -> 36.9 us
  starting transfers between devices: 205 us -> 92.9 us
  matrix products: 111 us -> 10.2 us
  Pallas kernels: 0 us -> 66.3 us
  between operations: 13.5 us -> 0.57 us
    ppermute x12 -> x27, waiting for transfers between devices: 268 us -> 32.4 us  [the longest x7 22.5 us: on_device(): pieces.append(lax.ppermute(blocks[index], 'frame', reach(back)))]
    while x25 -> x0, local copies, waits for them, and re-layouts: 117 us -> none
    ppermute x12 -> x27, starting transfers between devices: 205 us -> 92.9 us  [the longest x7 43.3 us: on_device(): pieces.append(lax.ppermute(blocks[index], 'frame', reach(back)))]
    reduce_scatter x1 -> x0, waiting for transfers between devices: 107 us -> none  [on_device(): lax.psum_scatter(jnp.dot(heads_out, out_weight, preferred_element_type=jn...]
    dot_general x9 -> x2, matrix products: 88.2 us -> 10.2 us  [the longest x1 6.13 us: on_device(): kept = jnp.dot(ours, weight, preferred_element_type=jnp.float32)]
    pallas_call x0 -> x2, Pallas kernels: none -> 66.3 us  [the longest x1 36.9 us: outer(): pl.pallas_call(functools.partial(outer_kernel, counts), grid_spec=pltpu.P...]
    gather x8 -> x10, local copies, waits for them, and re-layouts: 77.3 us -> 13.9 us  [the longest x7 12.1 us: on_device(): pieces.append(lax.ppermute(blocks[index], 'frame', reach(back)))]
    unnamed x18 -> x50, local copies, waits for them, and re-layouts: 39.4 us -> 1.44 us
  transfers between devices with their start and end apart: 13 -> 27, of which waited for: 5 -> 5; matrix products, arithmetic and copies ran while one was open for 5% -> 22% of each run, Pallas kernels for 0% -> 11%
where the time goes in v1:
time: 266 us; the launch traced here: 265 us
  starting transfers between devices  92.9 us (35%)
  Pallas kernels  66.3 us (25%)
  local copies, waits for them, and re-layouts  36.9 us (14%)
  waiting for transfers between devices  32.4 us (12%)
  other arithmetic  25.7 us (10%)
  matrix products  10.2 us (4%)
    ppermute x7, starting transfers between devices, on_device(): pieces.append(lax.ppermute(blocks[index], 'frame', reach(back)))  43.3 us
    pallas_call x1, Pallas kernels, outer(): pl.pallas_call(functools.partial(outer_kernel, counts), grid_spec=pltpu.P...  36.9 us
    pallas_call x1, Pallas kernels, inner(): pl.pallas_call(inner_kernel, grid=(heads,), in_specs=[column, column, pl....  29.5 us
    ppermute x7, starting transfers between devices, on_device(): asked = lax.ppermute(w, 'frame', reach(d))  23.2 us
    ppermute x7, waiting for transfers between devices, on_device(): pieces.append(lax.ppermute(blocks[index], 'frame', reach(back)))  22.5 us
    ppermute x12, starting transfers between devices, line(): return lax.ppermute(value, 'frame', line_pairs(n, shift))  14.7 us
    gather x7, local copies, waits for them, and re-layouts, on_device(): pieces.append(lax.ppermute(blocks[index], 'frame', reach(back)))  12.1 us
    ppermute x1, starting transfers between devices, on_device(): other = lax.ppermute(sent, 'head', [(0, 1), (1, 0)])  11.7 us
  transfers between devices with their start and end apart: 27, of which 5 were waited for; matrix products, arithmetic and copies ran while one was open for 22% of the time, Pallas kernels for 11%

profile of v1, /device:TPU:1, one launch (start us, length us, event | category | flops | bytes accessed | tf_op | source)
XLA Modules:
  0.0 265.0 jit_solution(6286043781062312885)
XLA Ops:
  0.0 2.1 collective-permute-start
  2.1 2.6 collective-permute-start.1
  5.8 2.2 constant_dynamic-slice_fusion.10
  22.2 1.7 collective-permute-start.8
  25.9 5.5 %collective-permute-start.15 = (s32[8]{0:T(128)S(1)}, s32[8]{0:T(128)S(1)}, u32[]{:S(2)}, u32[]{:S(2)}) collective-permute-start(s32[8]{0:T(128)S(1)} %reshape_squeeze.13), channel_id=1, source_target_pairs={{0,16},{2,18},{4,20},{6,22},{8,24},{10,26},{12,28},{14,30},{16,32}... | collective-permute-start | bytes 104 | tf_op jit(solution)/shard_map/ppermute | solution.py:231
  38.0 2.1 and_reduce_fusion
  42.1 4.0 %collective-permute-start.11 = (s32[18]{0:T(128)S(1)}, s32[18]{0:T(128)S(1)}, u32[]{:S(2)}, u32[]{:S(2)}) collective-permute-start(s32[18]{0:T(128)S(1)} %concatenate.93), channel_id=1, source_target_pairs={{0,8},{2,10},{4,12},{6,14},{8,16},{10,18},{12,20},{14,22},{16,24},... | collective-permute-start | bytes 224 | tf_op jit(solution)/shard_map/ppermute | solution.py:231
  47.8 1.8 collective-permute-start.4
  50.8 6.7 %collective-permute-start.19 = (s32[8]{0:T(128)}, s32[8]{0:T(128)}, u32[]{:S(2)}, u32[]{:S(2)}) collective-permute-start(s32[8]{0:T(128)} %reshape_squeeze.15), channel_id=1, source_target_pairs={{0,32},{2,34},{4,36},{6,38},{8,40},{10,42},{12,44},{14,46},{16,48}... | collective-permute-start | bytes 104 | tf_op jit(solution)/shard_map/ppermute | solution.py:231
  57.6 3.1 %collective-permute-start.21 = (s32[8]{0:T(128)}, s32[8]{0:T(128)}, u32[]{:S(2)}, u32[]{:S(2)}) collective-permute-start(s32[8]{0:T(128)} %max.58), channel_id=1, source_target_pairs={{0,64},{2,66},{4,68},{6,70},{8,72},{10,74},{12,76},{14,78},{16,80}... | collective-permute-start | bytes 104 | tf_op jit(solution)/shard_map/ppermute | solution.py:231
  62.0 2.0 pad_maximum_fusion.1
  64.1 2.2 gather_fusion.2
  66.3 2.2 gather_fusion.3
  68.5 1.6 gather_fusion.5
  70.1 1.6 gather_fusion.6
  71.7 2.5 collective-permute-start.10
  76.8 9.7 %collective-permute-start.18 = (bf16[8,64,768]{2,1,0:T(8,128)(2,1)}, bf16[8,64,768]{2,1,0:T(8,128)(2,1)}, u32[]{:S(2)}, u32[]{:S(2)}) collective-permute-start(bf16[8,64,768]{2,1,0:T(8,128)(2,1)} %gather_fusion.6), channel_id=1, source_target_pairs={{0,32},{2,34},{4,36},{6,38},{8,40},{10,42},{12,44},{14,46},{16,48}... | collective-permute-start | bytes 2359304 | tf_op jit(solution)/shard_map/ppermute | solution.py:235
  88.7 2.1 broadcast_in_dim_reshape.5.bias_ref
  92.7 2.0 broadcast_in_dim_reshape.12.bias_ref
  105.3 22.4 %collective-permute-done.16.rest_3_ = bf16[8,64,768]{2,1,0:T(8,128)(2,1)} collective-permute-done((bf16[8,64,768]{2,1,0:T(8,128)(2,1)}, bf16[8,64,768]{2,1,0:T(8,128)(2,1)}, u32[]{:S(2)}, u32[]{:S(2)}) %collective-permute-start.16) | collective-permute-done | bytes 786464 | tf_op jit(solution)/shard_map/ppermute | solution.py:235
  127.8 19.8 %collective-permute-start.22 = (bf16[8,64,768]{2,1,0:T(8,128)(2,1)}, bf16[8,64,768]{2,1,0:T(8,128)(2,1)S(1)}, u32[]{:S(2)}, u32[]{:S(2)}) collective-permute-start(bf16[8,64,768]{2,1,0:T(8,128)(2,1)} %gather_fusion.8), channel_id=1, source_target_pairs={{0,64},{2,66},{4,68},{6,70},{8,72},{10,74},{12,76},{14,78},{16,80}... | collective-permute-start | bytes 2359304 | tf_op jit(solution)/shard_map/ppermute | solution.py:235
  147.6 7.4 %collective-permute-start.14 = (bf16[8,64,768]{2,1,0:T(8,128)(2,1)}, bf16[8,64,768]{2,1,0:T(8,128)(2,1)S(1)}, u32[]{:S(2)}, u32[]{:S(2)}) collective-permute-start(bf16[8,64,768]{2,1,0:T(8,128)(2,1)} %gather_fusion.4), channel_id=1, source_target_pairs={{0,16},{2,18},{4,20},{6,22},{8,24},{10,26},{12,28},{14,30},{16,32}... | collective-permute-start | bytes 2359304 | tf_op jit(solution)/shard_map/ppermute | solution.py:235
  155.1 2.5 pad_maximum_fusion.4.q_ref
  157.6 29.5 %shard_map.55 = (f32[2048,384]{1,0:T(8,128)}, f32[2048,384]{1,0:T(8,128)}, f32[2048,384]{1,0:T(8,128)}) custom-call(bf16[2048,384]{1,0:T(8,128)(2,1)} %pad_maximum_fusion.4.q_ref, bf16[2048,768]{1,0:T(8,128)(2,1)} %bitcast.74, bf16[2048,768]{1,0:T(8,128)(2,1)} %bitcast.75, f32[32,1,2048]{2,1,0:T(1,128)} %broadcast_in_dim_reshape.5.bias_ref), custom_call_target="tpu_custom_call" | custom-call | flops 6442450944 | bytes 12582912 | tf_op jit(solution)/shard_map/pallas_call | solution.py:72
  188.5 36.9 %shard_map.56 = bf16[2048,384]{1,0:T(8,128)(2,1)} custom-call(s32[104]{0:T(128)} %max.56.table, bf16[2048,384]{1,0:T(8,128)(2,1)} %pad_maximum_fusion.4.q_ref, f32[32,1,1664]{2,1,0:T(1,128)} %broadcast_in_dim_reshape.12.bias_ref, f32[2048,384]{1,0:T(8,128)} %get-tuple-element.8.acc_ref, f32[2048,384]{1,0:T(8,128)} %get-tuple-element.9.peak_ref, ...), custom_call_target="tpu_custom_call" | custom-call | flops 5234491392 | bytes 12582912 | tf_op jit(solution)/shard_map/pallas_call | solution.py:136
  226.9 1.9 collective-permute-start.24
  229.9 4.6 %constant_dynamic-slice_fusion.3 = (bf16[384,3072]{1,0:T(8,128)(2,1)S(1)}, bf16[384,3072]{1,0:T(8,128)(2,1)S(1)}, bf16[384,3072]{1,0:T(8,128)(2,1)S(1)}, bf16[384,3072]{1,0:T(8,128)(2,1)S(1)}) fusion(bf16[1536,3072]{1,0:T(8,128)(2,1)} %param.9, s32[]{:T(128)S(6)} %select_n.292, s32[]{:T(128)S(6)} %select_n.339, s32[]{:T(128)S(6)} %select_n.341, s32[]{:T(128)S(6)} %select_n.340), kind=kLoop, calls=%fused_computation.31 | loop fusion | bytes 18874384 | tf_op jit(solution)/shard_map/dynamic_slice | solution.py:275
  234.5 4.5 %collective-permute-done.23 = bf16[512,384]{1,0:T(8,128)(2,1)S(1)} collective-permute-done((bf16[512,384]{1,0:T(8,128)(2,1)S(1)}, bf16[512,384]{1,0:T(8,128)(2,1)S(1)}, u32[]{:S(2)}, u32[]{:S(2)}) %collective-permute-start.23) | collective-permute-done | bytes 393248 | tf_op jit(solution)/shard_map/ppermute | solution.py:212
  239.8 4.1 %convolution_convert_fusion = bf16[256,3072]{1,0:T(8,128)(2,1)} fusion(bf16[384,3072]{1,0:T(8,128)(2,1)S(1)} %get-tuple-element.22, bf16[384,3072]{1,0:T(8,128)(2,1)S(1)} %get-tuple-element.23, bf16[384,3072]{1,0:T(8,128)(2,1)S(1)} %get-tuple-element.21, bf16[384,3072]{1,0:T(8,128)(2,1)S(1)} %get-tuple-element.20, ...), kind=kOutput, calls=%fused_computation.11 | convolution fusion | flops 2454454272 | bytes 11796484 | tf_op jit(solution)/shard_map/dot_general | solution.py:281
  243.8 11.7 %collective-permute-start.26 = (bf16[256,3072]{1,0:T(8,128)(2,1)}, bf16[256,3072]{1,0:T(8,128)(2,1)}, u32[]{:S(2)}, u32[]{:S(2)}) collective-permute-start(bf16[256,3072]{1,0:T(8,128)(2,1)} %convolution_convert_fusion), channel_id=1, source_target_pairs={{0,1},{1,0},{2,3},{3,2},{4,5},{5,4},{6,7},{7,6},{8,9},{9,8},{10,11... | collective-permute-start | bytes 4718600 | tf_op jit(solution)/shard_map/ppermute | solution.py:282
  255.5 3.4 %collective-permute-done.26 = bf16[256,3072]{1,0:T(8,128)(2,1)} collective-permute-done((bf16[256,3072]{1,0:T(8,128)(2,1)}, bf16[256,3072]{1,0:T(8,128)(2,1)}, u32[]{:S(2)}, u32[]{:S(2)}) %collective-permute-start.26) | collective-permute-done | bytes 1572896 | tf_op jit(solution)/shard_map/ppermute | solution.py:282
  258.9 6.1 %fusion = bf16[256,3072]{1,0:T(8,128)(2,1)} fusion(bf16[256,3072]{1,0:T(8,128)(2,1)} %collective-permute-done.26, bf16[384,3072]{1,0:T(8,128)(2,1)} %copy-done.2, bf16[384,3072]{1,0:T(8,128)(2,1)} %copy-done.3, bf16[384,3072]{1,0:T(8,128)(2,1)} %copy-done.1, bf16[384,3072]{1,0:T(8,128)(2,1)S(1)} %get-tuple-element.20, bf16[512,1536]{1,0:T(8,128)(2,1)} %copy-done.4, ...), kind=kOutput, calls=%fused_computation.12 | convolution fusion | flops 2456027136 | bytes 13369348 | tf_op jit(solution)/shard_map/dot_general | solution.py:283
  (184 shorter events, 51.9 us)
Async XLA Ops:
  0.0 22.2 %collective-permute-start = (s32[8,32]{1,0:T(8,128)}, s32[8,32]{1,0:T(8,128)S(1)}, u32[]{:S(2)}, u32[]{:S(2)}) collective-permute-start(s32[8,32]{1,0:T(8,128)} %param.8), channel_id=1, source_target_pairs={{0,2},{2,4},{4,6},{6,0},{8,10},{10,12},{12,14},{14,8},{16,18},{18,... | collective-permute-start | bytes 3080 | tf_op jit(solution)/shard_map/ppermute | solution.py:212
  2.1 21.7 %collective-permute-start.1 = (s32[8,32]{1,0:T(8,128)}, s32[8,32]{1,0:T(8,128)S(1)}, u32[]{:S(2)}, u32[]{:S(2)}) collective-permute-start(s32[8,32]{1,0:T(8,128)} %param.8), channel_id=1, source_target_pairs={{0,4},{2,6},{4,0},{6,2},{8,12},{10,14},{12,8},{14,10},{16,20},{18,... | collective-permute-start | bytes 3080 | tf_op jit(solution)/shard_map/ppermute | solution.py:212
  4.7 19.1 %collective-permute-start.2 = (s32[8,32]{1,0:T(8,128)}, s32[8,32]{1,0:T(8,128)S(1)}, u32[]{:S(2)}, u32[]{:S(2)}) collective-permute-start(s32[8,32]{1,0:T(8,128)} %param.8), channel_id=1, source_target_pairs={{0,6},{2,0},{4,2},{6,4},{8,14},{10,8},{12,10},{14,12},{16,22},{18,... | collective-permute-start | bytes 3080 | tf_op jit(solution)/shard_map/ppermute | solution.py:212
  9.0 41.9 %collective-permute-start.6 = (bf16[512,768]{1,0:T(8,128)(2,1)}, bf16[512,768]{1,0:T(8,128)(2,1)}, u32[]{:S(2)}, u32[]{:S(2)}) collective-permute-start(bf16[512,768]{1,0:T(8,128)(2,1)} %pad_maximum_fusion.6), channel_id=1, source_target_pairs={{0,2},{2,4},{4,6},{6,0},{8,10},{10,12},{12,14},{14,8},{16,18},{18,... | collective-permute-start | bytes 2359304 | tf_op jit(solution)/shard_map/ppermute | solution.py:212
  10.3 47.3 %collective-permute-start.7 = (bf16[512,768]{1,0:T(8,128)(2,1)}, bf16[512,768]{1,0:T(8,128)(2,1)}, u32[]{:S(2)}, u32[]{:S(2)}) collective-permute-start(bf16[512,768]{1,0:T(8,128)(2,1)} %pad_maximum_fusion.7), channel_id=1, source_target_pairs={{0,4},{2,6},{4,0},{6,2},{8,12},{10,14},{12,8},{14,10},{16,20},{18,... | collective-permute-start | bytes 2359304 | tf_op jit(solution)/shard_map/ppermute | solution.py:212
  19.4 15.4 %copy-start.12 = (s32[2]{0:T(128)S(1)}, s32[2]{0:T(128)}, u32[]{:S(2)}) copy-start(s32[2]{0:T(128)} %get-tuple-element.72) | copy-start | bytes 28
  19.4 15.4 %copy-start.13 = (s32[2]{0:T(128)S(1)}, s32[2]{0:T(128)}, u32[]{:S(2)}) copy-start(s32[2]{0:T(128)} %get-tuple-element.73) | copy-start | bytes 28
  19.4 15.4 %copy-start.14 = (s32[4]{0:T(128)S(1)}, s32[4]{0:T(128)}, u32[]{:S(2)}) copy-start(s32[4]{0:T(128)} %iota_add_fusion.12) | copy-start | bytes 52
  22.2 38.6 %collective-permute-start.8 = (bf16[512,768]{1,0:T(8,128)(2,1)S(1)}, bf16[512,768]{1,0:T(8,128)(2,1)S(1)}, u32[]{:S(2)}, u32[]{:S(2)}) collective-permute-start(bf16[512,768]{1,0:T(8,128)(2,1)S(1)} %pad_maximum_fusion.8), channel_id=1, source_target_pairs={{0,6},{2,0},{4,2},{6,4},{8,14},{10,8},{12,10},{14,12},{16,22},{18,... | collective-permute-start | bytes 2359304 | tf_op jit(solution)/shard_map/ppermute | solution.py:212
  25.9 14.8 %collective-permute-start.15 = (s32[8]{0:T(128)S(1)}, s32[8]{0:T(128)S(1)}, u32[]{:S(2)}, u32[]{:S(2)}) collective-permute-start(s32[8]{0:T(128)S(1)} %reshape_squeeze.13), channel_id=1, source_target_pairs={{0,16},{2,18},{4,20},{6,22},{8,24},{10,26},{12,28},{14,30},{16,32}... | collective-permute-start | bytes 104 | tf_op jit(solution)/shard_map/ppermute | solution.py:231
  31.5 10.5 %collective-permute-start.17 = (s32[8]{0:T(128)S(1)}, s32[8]{0:T(128)S(1)}, u32[]{:S(2)}, u32[]{:S(2)}) collective-permute-start(s32[8]{0:T(128)S(1)} %reshape_squeeze.14), channel_id=1, source_target_pairs={{32,0},{34,2},{36,4},{38,6},{40,8},{42,10},{44,12},{46,14},{48,16}... | collective-permute-start | bytes 104 | tf_op jit(solution)/shard_map/ppermute | solution.py:231
  38.0 24.0 %copy-start.10 = (s32[4,26]{1,0:T(4,128)}, s32[4,26]{1,0:T(4,128)S(1)}, u32[]{:S(2)}) copy-start(s32[4,26]{1,0:T(4,128)S(1)} %concatenate.78) | copy-start | bytes 1252
  40.8 6.5 %collective-permute-start.9 = (s32[18]{0:T(128)S(1)}, s32[18]{0:T(128)S(1)}, u32[]{:S(2)}, u32[]{:S(2)}) collective-permute-start(s32[18]{0:T(128)S(1)} %concatenate.92), channel_id=1, source_target_pairs={{8,0},{10,2},{12,4},{14,6},{16,8},{18,10},{20,12},{22,14},{24,16},... | collective-permute-start | bytes 224 | tf_op jit(solution)/shard_map/ppermute | solution.py:231
  42.1 5.7 %collective-permute-start.11 = (s32[18]{0:T(128)S(1)}, s32[18]{0:T(128)S(1)}, u32[]{:S(2)}, u32[]{:S(2)}) collective-permute-start(s32[18]{0:T(128)S(1)} %concatenate.93), channel_id=1, source_target_pairs={{0,8},{2,10},{4,12},{6,14},{8,16},{10,18},{12,20},{14,22},{16,24},... | collective-permute-start | bytes 224 | tf_op jit(solution)/shard_map/ppermute | solution.py:231
  47.3 29.5 %collective-permute-start.3 = (bf16[512,384]{1,0:T(8,128)(2,1)}, bf16[512,384]{1,0:T(8,128)(2,1)}, u32[]{:S(2)}, u32[]{:S(2)}) collective-permute-start(bf16[512,384]{1,0:T(8,128)(2,1)} %get-tuple-element.37), channel_id=1, source_target_pairs={{0,2},{2,4},{4,6},{6,0},{8,10},{10,12},{12,14},{14,8},{16,18},{18,... | collective-permute-start | bytes 1179656 | tf_op jit(solution)/shard_map/ppermute | solution.py:212
  47.8 49.0 %collective-permute-start.4 = (bf16[512,384]{1,0:T(8,128)(2,1)}, bf16[512,384]{1,0:T(8,128)(2,1)}, u32[]{:S(2)}, u32[]{:S(2)}) collective-permute-start(bf16[512,384]{1,0:T(8,128)(2,1)} %get-tuple-element.39), channel_id=1, source_target_pairs={{0,4},{2,6},{4,0},{6,2},{8,12},{10,14},{12,8},{14,10},{16,20},{18,... | collective-permute-start | bytes 1179656 | tf_op jit(solution)/shard_map/ppermute | solution.py:212
  50.8 20.8 %collective-permute-start.19 = (s32[8]{0:T(128)}, s32[8]{0:T(128)}, u32[]{:S(2)}, u32[]{:S(2)}) collective-permute-start(s32[8]{0:T(128)} %reshape_squeeze.15), channel_id=1, source_target_pairs={{0,32},{2,34},{4,36},{6,38},{8,40},{10,42},{12,44},{14,46},{16,48}... | collective-permute-start | bytes 104 | tf_op jit(solution)/shard_map/ppermute | solution.py:231
  57.6 16.6 %collective-permute-start.21 = (s32[8]{0:T(128)}, s32[8]{0:T(128)}, u32[]{:S(2)}, u32[]{:S(2)}) collective-permute-start(s32[8]{0:T(128)} %max.58), channel_id=1, source_target_pairs={{0,64},{2,66},{4,68},{6,70},{8,72},{10,74},{12,76},{14,78},{16,80}... | collective-permute-start | bytes 104 | tf_op jit(solution)/shard_map/ppermute | solution.py:231
  60.7 14.8 %collective-permute-start.13 = (s32[8]{0:T(128)}, s32[8]{0:T(128)}, u32[]{:S(2)}, u32[]{:S(2)}) collective-permute-start(s32[8]{0:T(128)} %reshape_squeeze.12), channel_id=1, source_target_pairs={{16,0},{18,2},{20,4},{22,6},{24,8},{26,10},{28,12},{30,14},{32,16}... | collective-permute-start | bytes 104 | tf_op jit(solution)/shard_map/ppermute | solution.py:231
  64.1 37.0 %copy-start = (bf16[4,512,768]{2,1,0:T(8,128)(2,1)}, bf16[4,512,768]{2,1,0:T(8,128)(2,1)S(1)}, u32[]{:S(2)}) copy-start(bf16[4,512,768]{2,1,0:T(8,128)(2,1)S(1)} %pad_maximum_fusion.1) | copy-start | bytes 9437188
  71.7 115.4 %collective-permute-start.10 = (bf16[18,64,768]{2,1,0:T(8,128)(2,1)}, bf16[18,64,768]{2,1,0:T(8,128)(2,1)}, u32[]{:S(2)}, u32[]{:S(2)}) collective-permute-start(bf16[18,64,768]{2,1,0:T(8,128)(2,1)} %gather_fusion.2), channel_id=1, source_target_pairs={{0,8},{2,10},{4,12},{6,14},{8,16},{10,18},{12,20},{14,22},{16,24},... | collective-permute-start | bytes 5308424 | tf_op jit(solution)/shard_map/ppermute | solution.py:235
  74.2 112.9 %collective-permute-start.12 = (bf16[18,64,768]{2,1,0:T(8,128)(2,1)}, bf16[18,64,768]{2,1,0:T(8,128)(2,1)}, u32[]{:S(2)}, u32[]{:S(2)}) collective-permute-start(bf16[18,64,768]{2,1,0:T(8,128)(2,1)} %gather_fusion.3), channel_id=1, source_target_pairs={{8,0},{10,2},{12,4},{14,6},{16,8},{18,10},{20,12},{22,14},{24,16},... | collective-permute-start | bytes 5308424 | tf_op jit(solution)/shard_map/ppermute | solution.py:235
  75.5 52.3 %collective-permute-start.16 = (bf16[8,64,768]{2,1,0:T(8,128)(2,1)}, bf16[8,64,768]{2,1,0:T(8,128)(2,1)}, u32[]{:S(2)}, u32[]{:S(2)}) collective-permute-start(bf16[8,64,768]{2,1,0:T(8,128)(2,1)} %gather_fusion.5), channel_id=1, source_target_pairs={{16,0},{18,2},{20,4},{22,6},{24,8},{26,10},{28,12},{30,14},{32,16}... | collective-permute-start | bytes 2359304 | tf_op jit(solution)/shard_map/ppermute | solution.py:235
  76.8 70.8 %collective-permute-start.18 = (bf16[8,64,768]{2,1,0:T(8,128)(2,1)}, bf16[8,64,768]{2,1,0:T(8,128)(2,1)}, u32[]{:S(2)}, u32[]{:S(2)}) collective-permute-start(bf16[8,64,768]{2,1,0:T(8,128)(2,1)} %gather_fusion.6), channel_id=1, source_target_pairs={{0,32},{2,34},{4,36},{6,38},{8,40},{10,42},{12,44},{14,46},{16,48}... | collective-permute-start | bytes 2359304 | tf_op jit(solution)/shard_map/ppermute | solution.py:235
  96.7 7.3 %collective-permute-start.5 = (bf16[512,384]{1,0:T(8,128)(2,1)}, bf16[512,384]{1,0:T(8,128)(2,1)}, u32[]{:S(2)}, u32[]{:S(2)}) collective-permute-start(bf16[512,384]{1,0:T(8,128)(2,1)} %get-tuple-element.38), channel_id=1, source_target_pairs={{0,6},{2,0},{4,2},{6,4},{8,14},{10,8},{12,10},{14,12},{16,22},{18,... | collective-permute-start | bytes 1179656 | tf_op jit(solution)/shard_map/ppermute | solution.py:212
  104.0 83.0 %collective-permute-start.20 = (bf16[8,64,768]{2,1,0:T(8,128)(2,1)}, bf16[8,64,768]{2,1,0:T(8,128)(2,1)S(1)}, u32[]{:S(2)}, u32[]{:S(2)}) collective-permute-start(bf16[8,64,768]{2,1,0:T(8,128)(2,1)} %gather_fusion.7), channel_id=1, source_target_pairs={{32,0},{34,2},{36,4},{38,6},{40,8},{42,10},{44,12},{46,14},{48,16}... | collective-permute-start | bytes 2359304 | tf_op jit(solution)/shard_map/ppermute | solution.py:235
  127.8 59.3 %collective-permute-start.22 = (bf16[8,64,768]{2,1,0:T(8,128)(2,1)}, bf16[8,64,768]{2,1,0:T(8,128)(2,1)S(1)}, u32[]{:S(2)}, u32[]{:S(2)}) collective-permute-start(bf16[8,64,768]{2,1,0:T(8,128)(2,1)} %gather_fusion.8), channel_id=1, source_target_pairs={{0,64},{2,66},{4,68},{6,70},{8,72},{10,74},{12,76},{14,78},{16,80}... | collective-permute-start | bytes 2359304 | tf_op jit(solution)/shard_map/ppermute | solution.py:235
  147.6 39.5 %collective-permute-start.14 = (bf16[8,64,768]{2,1,0:T(8,128)(2,1)}, bf16[8,64,768]{2,1,0:T(8,128)(2,1)S(1)}, u32[]{:S(2)}, u32[]{:S(2)}) collective-permute-start(bf16[8,64,768]{2,1,0:T(8,128)(2,1)} %gather_fusion.4), channel_id=1, source_target_pairs={{0,16},{2,18},{4,20},{6,22},{8,24},{10,26},{12,28},{14,30},{16,32}... | collective-permute-start | bytes 2359304 | tf_op jit(solution)/shard_map/ppermute | solution.py:235
  226.9 12.1 %collective-permute-start.23 = (bf16[512,384]{1,0:T(8,128)(2,1)S(1)}, bf16[512,384]{1,0:T(8,128)(2,1)S(1)}, u32[]{:S(2)}, u32[]{:S(2)}) collective-permute-start(bf16[512,384]{1,0:T(8,128)(2,1)S(1)} %get-tuple-element.27), channel_id=1, source_target_pairs={{0,2},{2,4},{4,6},{6,0},{8,10},{10,12},{12,14},{14,8},{16,18},{18,... | collective-permute-start | bytes 1179656 | tf_op jit(solution)/shard_map/ppermute | solution.py:212
  226.9 12.0 %collective-permute-start.24 = (bf16[512,384]{1,0:T(8,128)(2,1)S(1)}, bf16[512,384]{1,0:T(8,128)(2,1)S(1)}, u32[]{:S(2)}, u32[]{:S(2)}) collective-permute-start(bf16[512,384]{1,0:T(8,128)(2,1)S(1)} %get-tuple-element.26), channel_id=1, source_target_pairs={{0,4},{2,6},{4,0},{6,2},{8,12},{10,14},{12,8},{14,10},{16,20},{18,... | collective-permute-start | bytes 1179656 | tf_op jit(solution)/shard_map/ppermute | solution.py:212
  228.9 10.7 %collective-permute-start.25 = (bf16[512,384]{1,0:T(8,128)(2,1)S(1)}, bf16[512,384]{1,0:T(8,128)(2,1)S(1)}, u32[]{:S(2)}, u32[]{:S(2)}) collective-permute-start(bf16[512,384]{1,0:T(8,128)(2,1)S(1)} %get-tuple-element.25), channel_id=1, source_target_pairs={{0,6},{2,0},{4,2},{6,4},{8,14},{10,8},{12,10},{14,12},{16,22},{18,... | collective-permute-start | bytes 1179656 | tf_op jit(solution)/shard_map/ppermute | solution.py:212
  243.8 15.1 %collective-permute-start.26 = (bf16[256,3072]{1,0:T(8,128)(2,1)}, bf16[256,3072]{1,0:T(8,128)(2,1)}, u32[]{:S(2)}, u32[]{:S(2)}) collective-permute-start(bf16[256,3072]{1,0:T(8,128)(2,1)} %convolution_convert_fusion), channel_id=1, source_target_pairs={{0,1},{1,0},{2,3},{3,2},{4,5},{5,4},{6,7},{7,6},{8,9},{9,8},{10,11... | collective-permute-start | bytes 4718600 | tf_op jit(solution)/shard_map/ppermute | solution.py:282
  (20 other events, 157.8 us)
